TPU v7x, 256 devices: a whole 4x4x8 slice. The times are simulated.
256 devices in a mesh: dp: 8 (over x, core), tm: 8 (over z), space: 4 (over y).
Axes of the slice: x: 4, y: 4, z: 8, core: 2. Of those that a mesh axis runs over, the one named last changes fastest.
Arguments:
- latents: bfloat16 [8, 16, 8, 128, 512], P('dp', 'tm', 'space'), may hold values from -400 to 400
- owner: int32 [8, 4, 1], P('dp'), may hold values from 0 to 3; in each aligned block of 4 rows (0 to 3, 4 to 7, ..., all dimensions but the last counted through in order) at most 2 rows name the same one
- gamma: float32 [512], replicated, may hold values from 0.25 to 1.75
- beta: float32 [512], replicated, may hold values from -3 to 3
- weight: bfloat16 [512, 27, 256], P(('dp', 'tm', 'space')), may hold values from -0.0546875 to 0.0546875
- upstream: bfloat16 [8, 16, 4, 512, 256], P('dp', 'tm', 'space'), may hold values from -20 to 20
Outputs:
- dlatents: bfloat16 [8, 16, 8, 128, 512], P('dp', 'tm', 'space')
- dweight: float32 [512, 27, 256], P(('dp', 'tm', 'space'))
- dgamma: float32 [512], replicated
- dbeta: float32 [512], replicated
Inputs may be any that keep to these rules, and one draw needn't show every extreme that they name: `owner`: in every clip each of the 4 owners is named by at most 2 of the 4 tiles, and by exactly 2 in some clips.
All inputs are finite; a program needn't handle non-finite values.
Results may differ from a plain program's by a relative error of at most 0.002.
The roundings to bfloat16 on the way count: a program that leaves them out, or rounds other values in their place, can miss the bound.
Values may be sent and summed in bfloat16 or wider, within the bound.
A program may use at most 128 MiB of HBM per device.

v0:
```python
import math
import jax
import jax.numpy as jnp
from jax import lax
from jax.sharding import PartitionSpec as P

GROUPS = 32
TH = 8
TW = 16
EPS = 1e-06


def shifted(value, axis, steps):
    count = lax.axis_size(axis)
    initial, last = (max(0, -steps), min(count, count - steps))
    return lax.ppermute(value, axis, [(source, source + steps) for source in range(initial, last)])


def tap_list():
    return [(kt, ky, kx) for kt in range(3) for ky in range(3) for kx in range(3)]


def conv_grads(hidden, grads, weight, rscale):
    frames, count, cells, chans = hidden.shape
    outs_ch = grads.shape[3]
    first_dev = lax.axis_index("tm") == 0
    cache = shifted(hidden, "tm", 1)
    repeat = jnp.concatenate([hidden[:1], hidden[:1]], axis=0)
    cache = jnp.where(first_dev, repeat, cache)
    extended = jnp.concatenate([cache, hidden], axis=0).reshape(frames + 2, count, TH, TW, chans)
    padded = jnp.pad(extended, ((0, 0), (0, 0), (1, 1), (1, 1), (0, 0)))
    rows = grads.reshape(frames * count * cells, outs_ch)
    span = lax.axis_size(("dp", "tm", "space")) * weight.shape[0]
    terms = []
    for kt, ky, kx in tap_list():
        tap = padded[kt : kt + frames, :, ky : ky + TH, kx : kx + TW].reshape(
            frames * count * cells, span
        )
        terms.append(
            lax.dot_general(tap, rows, (((0,), (0,)), ((), ())), preferred_element_type=jnp.float32)
        )
    dweight = lax.psum_scatter(
        jnp.stack(terms, axis=1) * rscale, ("dp", "tm", "space"), scatter_dimension=0, tiled=True
    )
    piece = lax.all_gather(weight, ("dp", "tm", "space"), axis=0, tiled=True)
    span = piece.shape[0]
    total = jnp.zeros((frames + 2, count, TH + 2, TW + 2, span), jnp.float32)
    for index, (kt, ky, kx) in enumerate(tap_list()):
        back = lax.dot_general(
            rows, piece[:, index, :], (((1,), (1,)), ((), ())), preferred_element_type=jnp.float32
        )
        total = total.at[kt : kt + frames, :, ky : ky + TH, kx : kx + TW].add(
            back.reshape(frames, count, TH, TW, span)
        )
    dextended = total[:, :, 1 : TH + 1, 1 : TW + 1].reshape(frames + 2, count, cells, span)
    carried = shifted(dextended[:2].astype(jnp.bfloat16), "tm", -1).astype(jnp.float32)
    own_part = dextended[2:]
    own_part = own_part.at[frames - 2 :].add(carried)
    own_part = own_part.at[0].add(jnp.where(first_dev, dextended[0] + dextended[1], 0.0))
    return (own_part, dweight)


def shards(latents, owner, gamma, beta, weight, upstream):
    blocks = latents[0]
    frames, cap, cells, chans = blocks.shape
    spaces = lax.axis_size("space")
    here = lax.axis_index("space")
    per_dev = upstream.shape[2]
    outs_ch = upstream.shape[4]
    tile_ids = owner[0, :, 0]
    tiles = tile_ids.shape[0]
    width = chans // GROUPS
    hot = (tile_ids[:, None] == jnp.arange(spaces, dtype=jnp.int32)[None, :]).astype(jnp.int32)
    rank = jnp.sum((jnp.cumsum(hot, axis=0) - hot) * hot, axis=1)
    slot = tile_ids * cap + rank
    holds = slot[None, :] == (here * cap + jnp.arange(cap, dtype=jnp.int32))[:, None]
    live = jnp.any(holds, axis=1).astype(jnp.float32)
    tile_of = jnp.sum(holds.astype(jnp.int32) * jnp.arange(tiles, dtype=jnp.int32)[None, :], axis=1)
    frames_all = frames * lax.axis_size("tm")
    count = float(frames_all * tiles * cells * width)
    rscale = 1.0 / math.sqrt(lax.axis_size("dp") * frames_all * tiles * cells)
    values = blocks.astype(jnp.float32).reshape(frames, cap, cells, GROUPS, width)
    live_mask = live[None, :, None, None, None]
    total = lax.psum(jnp.sum(values * live_mask, axis=(0, 1, 2, 4)), ("tm", "space"))
    mean = total / count
    centred = values - mean[:, None]
    spread = lax.psum(jnp.sum(centred * centred * live_mask, axis=(0, 1, 2, 4)), ("tm", "space"))
    var = spread / count
    inverse = lax.rsqrt(var + EPS)
    normed = (centred * inverse[:, None]).reshape(frames, cap, cells, chans)
    act = normed * gamma + beta
    sig = jax.nn.sigmoid(act)
    hidden = (act * sig).astype(jnp.bfloat16)
    ups = upstream[0].astype(jnp.float32).reshape(frames, per_dev, TH, 2, TW, 2, outs_ch)
    pooled = jnp.sum(ups, axis=(3, 5)).reshape(frames, per_dev, cells, outs_ch).astype(jnp.bfloat16)
    all_pooled = lax.all_gather(pooled, "space", axis=1, tiled=True)
    live_slot = live[None, :, None, None] > 0.5
    grads = jnp.where(live_slot, all_pooled[:, tile_of], jnp.zeros((), jnp.bfloat16))
    dhidden, dweight = conv_grads(hidden, grads, weight, rscale)
    dact = dhidden * (sig * (1.0 + act * (1.0 - sig))) * live[None, :, None, None]
    dgamma, dbeta = lax.psum(
        (jnp.sum(dact * normed, axis=(0, 1, 2)) * rscale, jnp.sum(dact, axis=(0, 1, 2)) * rscale),
        ("dp", "tm", "space"),
    )
    dnorm = (dact * gamma).reshape(frames, cap, cells, GROUPS, width)
    ngroup = normed.reshape(frames, cap, cells, GROUPS, width)
    first_m, second_m = lax.psum(
        (jnp.sum(dnorm, axis=(0, 1, 2, 4)), jnp.sum(dnorm * ngroup, axis=(0, 1, 2, 4))),
        ("tm", "space"),
    )
    dvalues = inverse[:, None] * (
        dnorm - (first_m / count)[:, None] - ngroup * (second_m / count)[:, None]
    )
    dfull = dvalues.reshape(frames, cap, cells, chans)
    resid = jnp.pad(grads.astype(jnp.float32), ((0, 0), (0, 0), (0, 0), (0, chans - outs_ch)))
    dlatent = ((dfull + resid) * live[None, :, None, None]).astype(jnp.bfloat16)
    return (dlatent[None], dweight, dgamma, dbeta)


def solution(mesh):
    return jax.shard_map(
        shards,
        mesh=mesh,
        in_specs=(
            P("dp", "tm", "space", None, None),
            P("dp", None, None),
            P(),
            P(),
            P(("dp", "tm", "space"), None, None),
            P("dp", "tm", "space", None, None),
        ),
        out_specs=(
            P("dp", "tm", "space", None, None),
            P(("dp", "tm", "space"), None, None),
            P(),
            P(),
        ),
        check_vma=False,
    )
```

profile of v0, /device:TPU:2, one launch (start us, length us, event | category | flops | bytes accessed | tf_op | source)
XLA Modules:
  0.0 780.4 jit_solution(5624047049725243167)
XLA Ops:
  13.3 13.3 %all_gather.6 = bf16[2,4,128,256]{3,2,1,0:T(8,128)(2,1)S(1)} all-gather(bf16[2,1,128,256]{3,2,1,0:T(8,128)(2,1)S(1)} %bitcast.575), channel_id=1, replica_groups=mesh['dp'=8,'tm'=8,'space'=4] {'space'}, dimensions={1}, use_global_device_ids=true | all-gather | bytes 655360 | tf_op jit(solution)/shard_map/all_gather | solution.py:96
  29.4 78.8 %psum.42 = f32[32]{0:T(128)S(1)} all-reduce(f32[32]{0:T(128)S(1)} %reduce_sum.114), channel_id=1, replica_groups=mesh['dp'=8,'tm'=8,'space'=4] {'tm','space'}, use_global_device_ids=true, to_apply=%region_5.6 | all-reduce | flops 32 | bytes 256 | tf_op jit(solution)/shard_map/psum | solution.py:84
  110.6 22.7 %all-gather.2.cloned.1.call-done = bf16[512,27,256]{2,1,0:T(8,128)(2,1)} async-done(((bf16[2,27,256]{2,1,0:T(8,128)(2,1)}), bf16[512,27,256]{2,1,0:T(8,128)(2,1)}) %all-gather.2.cloned.1.call-update) | async-done | bytes 7077904 | tf_op jit(solution)/shard_map/all_gather | solution.py:45
  133.3 10.9 %fusion.73 = (bf16[512,1,256]{2,1,0:T(2,128)(2,1)S(1)}, bf16[512,1,256]{2,1,0:T(2,128)(2,1)S(1)}, bf16[512,1,256]{2,1,0:T(2,128)(2,1)}, bf16[512,1,256]{2,1,0:T(...) fusion(bf16[512,27,256]{2,1,0:T(8,128)(2,1)} %all-gather.2.clon, ...), kind=kLoop, calls=%fused_computation.207 | loop fusion | bytes 4194304 | tf_op jit(solution)/shard_map/slice | solution.py:50
  147.3 5.8 scatter-add.95
  155.0 5.8 scatter-add.96
  160.8 2.8 fusion.7
  165.5 5.8 scatter-add.100
  171.2 3.9 add_select_fusion
  175.1 7.1 scatter-add.101
  186.6 5.8 scatter-add.105
  192.4 21.0 %fusion.72 = (bf16[512,1,256]{2,1,0:T(2,128)(2,1)S(1)}, bf16[512,1,256]{2,1,0:T(2,128)(2,1)S(1)}, bf16[512,1,256]{2,1,0:T(2,128)(2,1)}, bf16[512,1,256]{2,1,0:T(...) fusion(bf16[512,27,256]{2,1,0:T(8,128)(2,1)} %all-gather.2.clon, ...), kind=kLoop, calls=%fused_computation.206 | loop fusion | bytes 9961472 | tf_op jit(solution)/shard_map/slice | solution.py:50
  215.1 5.8 scatter-add.106
  225.5 5.8 scatter-add.110
  233.2 5.8 scatter-add.111
  243.7 5.8 scatter-add.115
  251.4 6.0 scatter-add.116
  262.0 5.8 scatter-add.120
  269.6 5.8 scatter-add.121
  280.1 5.8 scatter-add.125
  287.8 5.8 scatter-add.126
  298.3 5.8 scatter-add.130
  306.0 5.8 scatter-add.131
  316.3 5.8 scatter-add.135
  323.9 5.8 scatter-add.136
  334.1 74.6 %psum.43 = f32[32]{0:T(128)S(1)} all-reduce(f32[32]{0:T(128)S(1)} %reduce_sum.117), channel_id=1, replica_groups=mesh['dp'=8,'tm'=8,'space'=4] {'tm','space'}, use_global_device_ids=true, to_apply=%region_8.9 | all-reduce | flops 32 | bytes 256 | tf_op jit(solution)/shard_map/psum | solution.py:87
  417.0 6.6 collective-permute-done.1
  427.1 3.1 pad_slice_fusion
  461.2 11.5 %broadcast_multiply_fusion = f32[512,27,256]{2,0,1:T(8,128)} fusion(f32[512,27,256]{2,0,1:T(8,128)} %fusion.9), kind=kLoop, calls=%fused_computation.25 | loop fusion | flops 3538944 | bytes 28311552 | tf_op jit(solution)/shard_map/mul | solution.py:43
  473.2 72.7 %all-reduce.5 = (f32[32]{0:T(128)S(1)}, f32[32]{0:T(128)S(1)}) all-reduce(f32[32]{0:T(128)S(1)} %reduce_sum.126, f32[32]{0:T(128)S(1)} %reduce_sum.123), channel_id=1, replica_groups=mesh['dp'=8,'tm'=8,'space'=4] {'tm','space'}, use_global_device_ids=true, to_apply=%region_17.18 | all-reduce | flops 64 | bytes 512 | tf_op jit(solution)/shard_map/psum | solution.py:107
  547.8 80.5 %all-reduce.4 = (f32[512]{0:T(512)}, f32[512]{0:T(512)}) all-reduce(f32[512]{0:T(512)S(1)} %get-tuple-element.442, f32[512]{0:T(512)S(1)} %get-tuple-element.441), channel_id=1, replica_groups=mesh['dp'=8,'tm'=8,'space'=4] {'dp','tm','space'}, use_global_device_ids=true, to_apply=%region_20.21 | all-reduce | flops 1024 | bytes 8192 | tf_op jit(solution)/shard_map/psum | solution.py:101
  628.2 143.5 %all-reduce.8.cloned.1.call-done = f32[512,27,256]{2,0,1:T(8,128)} async-done(((f32[512,27,256]{2,0,1:T(8,128)}), f32[512,27,256]{2,0,1:T(8,128)}) %all-reduce.8.cloned.1.call-update) | async-done | bytes 14155792
  (129 shorter events, 114.0 us)
Async XLA Ops:
  7.2 126.1 %all-gather.2.cloned.1.call-start = ((), (), s32[]{:S(2)}) async-start(), calls=%async_computation | async-start | bytes 8421376 | tf_op jit(solution)/shard_map/all_gather | solution.py:45
  8.6 763.1 %all-reduce.8.cloned.1.call-start = ((), (), s32[]{:S(2)}) async-start(), calls=%async_computation.1 | async-start | bytes 28311552
  323.9 90.0 %copy-start.1 = (f32[512]{0:T(512)S(1)}, f32[512]{0:T(512)}, u32[]{:S(2)}) copy-start(f32[512]{0:T(512)} %param.68) | copy-start | bytes 6148
  323.9 90.0 %copy-start.2 = (f32[512]{0:T(512)S(1)}, f32[512]{0:T(512)}, u32[]{:S(2)}) copy-start(f32[512]{0:T(512)} %param.69) | copy-start | bytes 6148
  332.3 80.3 %collective-permute-start = (bf16[2,2,128,512]{2,3,1,0:T(8,128)(2,1)}, bf16[2,2,128,512]{2,3,1,0:T(8,128)(2,1)}, u32[]{:S(2)}, u32[]{:S(2)}) collective-permute-start(bf16[2,2,128,512]{2,3,1,0:T(8,128)(2,1)} %copy.128), channel_id=1, source_target_pairs={{4,0},{8,4},{12,8},{16,12},{20,16},{24,20},{28,24},{5,1},{9,5},{13... | collective-permute-start | bytes 1572872 | tf_op jit(solution)/shard_map/ppermute | solution.py:16
  415.7 8.0 %collective-permute-start.1 = (bf16[2,2,128,512]{2,3,1,0:T(8,128)(2,1)S(1)}, bf16[2,2,128,512]{2,3,1,0:T(8,128)(2,1)S(1)}, u32[]{:S(2)}, u32[]{:S(2)}) collective-permute-start(bf16[2,2,128,512]{2,3,1,0:T(8,128)(2,1)S(1)} %get-tuple-element.436), channel_id=1, source_target_pairs={{0,4},{4,8},{8,12},{12,16},{16,20},{20,24},{24,28},{1,5},{5,9},{9,... | collective-permute-start | bytes 1572872 | tf_op jit(solution)/shard_map/ppermute | solution.py:16
  472.7 73.5 %copy-start = (f32[2,2,128,512]{2,3,1,0:T(8,128)S(1)}, f32[2,2,128,512]{2,3,1,0:T(8,128)}, u32[]{:S(2)}) copy-start(f32[2,2,128,512]{2,3,1,0:T(8,128)} %get-tuple-element.384) | copy-start | bytes 3145732
Sparse Core Ops, SparseCore 0:
  12.4 120.8 all-gather.1
  472.9 298.7 all-reduce.7
where the time goes:
time: 786 us; the launch traced here: 780 us
  blocking collectives  320 us (41%)
  waiting for transfers between devices  173 us (22%)
  local copies, waits for them, and re-layouts  159 us (20%)
  matrix products  87.1 us (11%)
  other arithmetic  24 us (3%)
  between operations  14.7 us (2%)
    unnamed x3, waiting for transfers between devices  144 us
    scatter-add x19, local copies, waits for them, and re-layouts, conv_grads(): total.at[kt:kt + frames, :, ky:ky + TH, kx:kx + TW]  108 us
    psum x1, blocking collectives, shards(): lax.psum((jnp.sum(dact * normed, axis=(0, 1, 2)) * rscale, jnp.sum(dact,...  80.5 us
    psum x1, blocking collectives, shards(): lax.psum(jnp.sum(values * live_mask, axis=(0, 1, 2, 4)), ('tm', 'space'))  78.8 us
    psum x1, blocking collectives, shards(): lax.psum(jnp.sum(centred * centred * live_mask, axis=(0, 1, 2, 4)), ('tm'...  74.6 us
    psum x1, blocking collectives, shards(): lax.psum((jnp.sum(dnorm, axis=(0, 1, 2, 4)), jnp.sum(dnorm * ngroup, axis...  72.7 us
    dot_general x27, matrix products, conv_grads(): lax.dot_general(rows, piece[:, index, :], (((1,), (1,)), ((), ())), prefe...  56.2 us
    slice x2, local copies, waits for them, and re-layouts, conv_grads(): piece[:, index, :]  31.9 us
  transfers between devices with their start and end apart: 4, of which 3 were waited for; matrix products, arithmetic and copies ran while one was open for 2% of the time, Pallas kernels for 0%

commit v1 on v0

--- a/solution.py
+++ b/solution.py
@@ -84,7 +84,9 @@
     total = lax.psum(jnp.sum(values * live_mask, axis=(0, 1, 2, 4)), ("tm", "space"))
     mean = total / count
     centred = values - mean[:, None]
-    spread = lax.psum(jnp.sum(centred * centred * live_mask, axis=(0, 1, 2, 4)), ("tm", "space"))
+    spread = lax.psum(
+        lax.psum(jnp.sum(centred * centred * live_mask, axis=(0, 1, 2, 4)), "space"), "tm"
+    )
     var = spread / count
     inverse = lax.rsqrt(var + EPS)
     normed = (centred * inverse[:, None]).reshape(frames, cap, cells, chans)

time: 786 us -> 735 us (0.935)
  blocking collectives: 320 us -> 266 us
    psum x1 -> x2, blocking collectives: 74.6 us -> 27.3 us  [the longest x1 17.7 us: shards(): lax.psum(lax.psum(jnp.sum(centred * centred * live_mask, axis=(0, 1, 2, 4...]
    psum x1, blocking collectives: 80.5 us -> 72 us  [shards(): lax.psum((jnp.sum(dact * normed, axis=(0, 1, 2)) * rscale, jnp.sum(dact,...]
where the time goes in v1:
time: 735 us; the launch traced here: 728 us
  blocking collectives  266 us (36%)
  waiting for transfers between devices  175 us (24%)
  local copies, waits for them, and re-layouts  159 us (22%)
  matrix products  87.1 us (12%)
  other arithmetic  24 us (3%)
  between operations  14.7 us (2%)
    unnamed x3, waiting for transfers between devices  146 us
    scatter-add x19, local copies, waits for them, and re-layouts, conv_grads(): total.at[kt:kt + frames, :, ky:ky + TH, kx:kx + TW]  108 us
    psum x1, blocking collectives, shards(): lax.psum(jnp.sum(values * live_mask, axis=(0, 1, 2, 4)), ('tm', 'space'))  78.8 us
    psum x1, blocking collectives, shards(): lax.psum((jnp.sum(dnorm, axis=(0, 1, 2, 4)), jnp.sum(dnorm * ngroup, axis...  74.4 us
    psum x1, blocking collectives, shards(): lax.psum((jnp.sum(dact * normed, axis=(0, 1, 2)) * rscale, jnp.sum(dact,...  72 us
    dot_general x27, matrix products, conv_grads(): lax.dot_general(rows, piece[:, index, :], (((1,), (1,)), ((), ())), prefe...  56.2 us
    slice x2, local copies, waits for them, and re-layouts, conv_grads(): piece[:, index, :]  31.9 us
    dot_general x27, matrix products, conv_grads(): lax.dot_general(tap, rows, (((0,), (0,)), ((), ())), preferred_element_ty...  31 us
  transfers between devices with their start and end apart: 4, of which 3 were waited for; matrix products, arithmetic and copies ran while one was open for 2% of the time, Pallas kernels for 0%

profile of v1, /device:TPU:2, one launch (start us, length us, event | category | flops | bytes accessed | tf_op | source)
XLA Modules:
  0.0 728.5 jit_solution(17461064628854679134)
XLA Ops:
  13.3 13.3 %all_gather.6 = bf16[2,4,128,256]{3,2,1,0:T(8,128)(2,1)S(1)} all-gather(bf16[2,1,128,256]{3,2,1,0:T(8,128)(2,1)S(1)} %bitcast.575), channel_id=1, replica_groups=mesh['dp'=8,'tm'=8,'space'=4] {'space'}, dimensions={1}, use_global_device_ids=true | all-gather | bytes 655360 | tf_op jit(solution)/shard_map/all_gather | solution.py:98
  29.4 78.8 %psum.49 = f32[32]{0:T(128)S(1)} all-reduce(f32[32]{0:T(128)S(1)} %reduce_sum.114), channel_id=1, replica_groups=mesh['dp'=8,'tm'=8,'space'=4] {'tm','space'}, use_global_device_ids=true, to_apply=%region_5.6 | all-reduce | flops 32 | bytes 256 | tf_op jit(solution)/shard_map/psum | solution.py:84
  110.6 22.7 %all-gather.2.cloned.1.call-done = bf16[512,27,256]{2,1,0:T(8,128)(2,1)} async-done(((bf16[2,27,256]{2,1,0:T(8,128)(2,1)}), bf16[512,27,256]{2,1,0:T(8,128)(2,1)}) %all-gather.2.cloned.1.call-update) | async-done | bytes 7077904 | tf_op jit(solution)/shard_map/all_gather | solution.py:45
  133.3 10.9 %fusion.73 = (bf16[512,1,256]{2,1,0:T(2,128)(2,1)S(1)}, bf16[512,1,256]{2,1,0:T(2,128)(2,1)S(1)}, bf16[512,1,256]{2,1,0:T(2,128)(2,1)}, bf16[512,1,256]{2,1,0:T(...) fusion(bf16[512,27,256]{2,1,0:T(8,128)(2,1)} %all-gather.2.clon, ...), kind=kLoop, calls=%fused_computation.207 | loop fusion | bytes 4194304 | tf_op jit(solution)/shard_map/slice | solution.py:50
  147.3 5.8 scatter-add.95
  155.0 5.8 scatter-add.96
  165.5 5.8 scatter-add.100
  171.2 3.9 add_select_fusion
  175.1 7.1 scatter-add.101
  186.6 5.8 scatter-add.105
  192.4 21.0 %fusion.72 = (bf16[512,1,256]{2,1,0:T(2,128)(2,1)S(1)}, bf16[512,1,256]{2,1,0:T(2,128)(2,1)S(1)}, bf16[512,1,256]{2,1,0:T(2,128)(2,1)}, bf16[512,1,256]{2,1,0:T(...) fusion(bf16[512,27,256]{2,1,0:T(8,128)(2,1)} %all-gather.2.clon, ...), kind=kLoop, calls=%fused_computation.206 | loop fusion | bytes 9961472 | tf_op jit(solution)/shard_map/slice | solution.py:50
  215.1 5.8 scatter-add.106
  225.5 5.8 scatter-add.110
  233.2 5.8 scatter-add.111
  243.7 5.8 scatter-add.115
  251.4 6.0 scatter-add.116
  262.0 5.8 scatter-add.120
  269.6 5.8 scatter-add.121
  280.1 5.8 scatter-add.125
  287.8 5.8 scatter-add.126
  298.3 5.8 scatter-add.130
  306.0 5.8 scatter-add.131
  316.3 5.8 scatter-add.135
  323.9 5.8 scatter-add.136
  334.1 9.5 %psum.50 = f32[32]{0:T(128)S(1)} all-reduce(f32[32]{0:T(128)S(1)} %reduce_sum.117), channel_id=1, replica_groups=mesh['dp'=8,'tm'=8,'space'=4] {'space'}, use_global_device_ids=true, to_apply=%region_8.9 | all-reduce | flops 32 | bytes 256 | tf_op jit(solution)/shard_map/psum | solution.py:88
  343.7 17.7 %psum.51 = f32[32]{0:T(128)S(1)} all-reduce(f32[32]{0:T(128)S(1)} %psum.50), channel_id=1, replica_groups=mesh['dp'=8,'tm'=8,'space'=4] {'tm'}, use_global_device_ids=true, to_apply=%region_9.10 | all-reduce | flops 32 | bytes 256 | tf_op jit(solution)/shard_map/psum | solution.py:87
  369.7 6.6 collective-permute-done.1
  379.7 3.1 pad_slice_fusion
  413.9 11.5 %broadcast_multiply_fusion = f32[512,27,256]{2,0,1:T(8,128)} fusion(f32[512,27,256]{2,0,1:T(8,128)} %fusion.9), kind=kLoop, calls=%fused_computation.25 | loop fusion | flops 3538944 | bytes 28311552 | tf_op jit(solution)/shard_map/mul | solution.py:43
  425.8 74.4 %all-reduce.5 = (f32[32]{0:T(128)S(1)}, f32[32]{0:T(128)S(1)}) all-reduce(f32[32]{0:T(128)S(1)} %reduce_sum.126, f32[32]{0:T(128)S(1)} %reduce_sum.123), channel_id=1, replica_groups=mesh['dp'=8,'tm'=8,'space'=4] {'tm','space'}, use_global_device_ids=true, to_apply=%region_18.19 | all-reduce | flops 64 | bytes 512 | tf_op jit(solution)/shard_map/psum | solution.py:109
  502.1 72.0 %all-reduce.4 = (f32[512]{0:T(512)}, f32[512]{0:T(512)}) all-reduce(f32[512]{0:T(512)S(1)} %get-tuple-element.442, f32[512]{0:T(512)S(1)} %get-tuple-element.441), channel_id=1, replica_groups=mesh['dp'=8,'tm'=8,'space'=4] {'dp','tm','space'}, use_global_device_ids=true, to_apply=%region_21.22 | all-reduce | flops 1024 | bytes 8192 | tf_op jit(solution)/shard_map/psum | solution.py:103
  574.0 145.8 %all-reduce.8.cloned.1.call-done = f32[512,27,256]{2,0,1:T(8,128)} async-done(((f32[512,27,256]{2,0,1:T(8,128)}), f32[512,27,256]{2,0,1:T(8,128)}) %all-reduce.8.cloned.1.call-update) | async-done | bytes 14155792
  (130 shorter events, 116.8 us)
Async XLA Ops:
  7.2 126.1 %all-gather.2.cloned.1.call-start = ((), (), s32[]{:S(2)}) async-start(), calls=%async_computation | async-start | bytes 8421376 | tf_op jit(solution)/shard_map/all_gather | solution.py:45
  8.6 711.2 %all-reduce.8.cloned.1.call-start = ((), (), s32[]{:S(2)}) async-start(), calls=%async_computation.1 | async-start | bytes 28311552
  323.9 42.7 %copy-start.1 = (f32[512]{0:T(512)S(1)}, f32[512]{0:T(512)}, u32[]{:S(2)}) copy-start(f32[512]{0:T(512)} %param.68) | copy-start | bytes 6148
  323.9 42.7 %copy-start.2 = (f32[512]{0:T(512)S(1)}, f32[512]{0:T(512)}, u32[]{:S(2)}) copy-start(f32[512]{0:T(512)} %param.69) | copy-start | bytes 6148
  332.3 33.0 %collective-permute-start = (bf16[2,2,128,512]{2,3,1,0:T(8,128)(2,1)}, bf16[2,2,128,512]{2,3,1,0:T(8,128)(2,1)}, u32[]{:S(2)}, u32[]{:S(2)}) collective-permute-start(bf16[2,2,128,512]{2,3,1,0:T(8,128)(2,1)} %copy.128), channel_id=1, source_target_pairs={{4,0},{8,4},{12,8},{16,12},{20,16},{24,20},{28,24},{5,1},{9,5},{13... | collective-permute-start | bytes 1572872 | tf_op jit(solution)/shard_map/ppermute | solution.py:16
  368.3 8.0 %collective-permute-start.1 = (bf16[2,2,128,512]{2,3,1,0:T(8,128)(2,1)S(1)}, bf16[2,2,128,512]{2,3,1,0:T(8,128)(2,1)S(1)}, u32[]{:S(2)}, u32[]{:S(2)}) collective-permute-start(bf16[2,2,128,512]{2,3,1,0:T(8,128)(2,1)S(1)} %get-tuple-element.436), channel_id=1, source_target_pairs={{0,4},{4,8},{8,12},{12,16},{16,20},{20,24},{24,28},{1,5},{5,9},{9,... | collective-permute-start | bytes 1572872 | tf_op jit(solution)/shard_map/ppermute | solution.py:16
  425.4 75.1 %copy-start = (f32[2,2,128,512]{2,3,1,0:T(8,128)S(1)}, f32[2,2,128,512]{2,3,1,0:T(8,128)}, u32[]{:S(2)}) copy-start(f32[2,2,128,512]{2,3,1,0:T(8,128)} %get-tuple-element.384) | copy-start | bytes 3145732
Sparse Core Ops, SparseCore 0:
  12.4 120.8 all-gather.1
  425.5 294.2 all-reduce.7
